TPU v7x, 32 devices: a whole 2x2x4 slice. The times are simulated.
32 devices in a mesh: ctx: 32 (over z, y, x, core).
Axes of the slice: x: 2, y: 2, z: 4, core: 2. Of those that a mesh axis runs over, the one named last changes fastest.
Arguments:
- tiles: bfloat16 [8192, 768], P('ctx'), may hold values from -6 to 6
- w_qkv: bfloat16 [768, 2304], replicated, may hold values from -1 to 1
- w_out: bfloat16 [768, 768], replicated, may hold values from -0.21875 to 0.21875
- cotangent: bfloat16 [8192, 768], P('ctx'), may hold values from -6 to 6
- offsets: int32 [2, 12], replicated, may hold values from 0 to 31, as said below
- pad_count: int32 [1], replicated, may hold values from 0 to 127
Outputs:
- out_rows: bfloat16 [8192, 768], P('ctx')
- grad_tiles: bfloat16 [8192, 768], P('ctx')
- grad_wqkv: float32 [768, 2304], P('ctx')
- grad_wout: float32 [768, 768], P('ctx')
Inputs may be any that keep to these rules, and one draw needn't show every extreme that they name: offsets[0, h] is below 8; offsets[1, h] is below 32.
All inputs are finite; a program needn't handle non-finite values.
Results may differ from a plain program's by a relative error of at most 0.033.
Values may be sent and summed in bfloat16 or wider, within the bound.
No kernel may reach another device: no remote copies, remote signals or barrier semaphores. Data moves between devices by JAX's collectives and lax.ppermute only.
A program may use at most 128 MiB of HBM per device.

v0:
```python
import jax
import jax.numpy as jnp
from jax import lax
from jax.sharding import PartitionSpec as P

D = 768
HEADS = 12
HEAD_DIM = 64
GROUP = 8
scale_factor = 0.125
block_rows = 512


def from_partner(value, axis, apart):
    mask = 2**apart
    pairs = [(source, source ^ mask) for source in range(lax.axis_size(axis))]
    return lax.ppermute(value, axis, pairs)


def pick_rows(array_in, stride, offsets_row):
    row_count = array_in.shape[0]
    blocked = array_in.reshape((row_count // stride, stride) + array_in.shape[1:])
    chosen = jnp.arange(stride, dtype=jnp.int32)[:, None] == offsets_row[None, :]
    chosen = chosen.reshape((1, stride, offsets_row.shape[0]) + (1,) * (array_in.ndim - 2))
    return jnp.sum(jnp.where(chosen, blocked, jnp.zeros((), array_in.dtype)), axis=1)


def spread_rows(array_in, stride, offsets_row, fill):
    chosen = jnp.arange(stride, dtype=jnp.int32)[:, None] == offsets_row[None, :]
    chosen = chosen.reshape((1, stride, offsets_row.shape[0]) + (1,) * (array_in.ndim - 2))
    widened = jnp.where(chosen, array_in[:, None], jnp.asarray(fill, array_in.dtype))
    return widened.reshape((array_in.shape[0] * stride,) + array_in.shape[1:])


def masked_scores(queries, key_rows, key_valid):
    scores = (
        jnp.einsum("nhe,mhe->hnm", queries, key_rows, preferred_element_type=jnp.float32)
        * scale_factor
    )
    return jnp.where(key_valid[:, None, :], scores, -jnp.inf)


def level_forward(queries, key_rows, value_rows, key_valid):
    scores = masked_scores(queries, key_rows, key_valid)
    peak = jnp.max(scores, axis=-1, keepdims=True)
    log_total = peak[..., 0] + jnp.log(jnp.sum(jnp.exp(scores - peak), axis=-1))
    weights = jnp.exp(scores - log_total[..., None]).astype(jnp.bfloat16)
    mixed = jnp.einsum("hnm,mhe->nhe", weights, value_rows, preferred_element_type=jnp.float32)
    return (mixed, log_total.T)


def level_grads(
    queries,
    key_rows,
    value_rows,
    key_valid,
    log_total,
    grad_out,
    delta_rows,
    want_queries,
    want_keys,
):
    scores = masked_scores(queries, key_rows, key_valid)
    probs = jnp.exp(scores - log_total.T[:, :, None])
    grad_probs = jnp.einsum(
        "nhe,mhe->hnm", grad_out, value_rows, preferred_element_type=jnp.float32
    )
    grad_scores = (probs * (grad_probs - delta_rows.T[:, :, None])).astype(jnp.bfloat16)
    results = []
    if want_queries:
        results.append(
            scale_factor
            * jnp.einsum("hnm,mhe->nhe", grad_scores, key_rows, preferred_element_type=jnp.float32)
        )
    if want_keys:
        results.append(
            scale_factor
            * jnp.einsum("hnm,nhe->mhe", grad_scores, queries, preferred_element_type=jnp.float32)
        )
        results.append(
            jnp.einsum(
                "hnm,nhe->mhe",
                probs.astype(jnp.bfloat16),
                grad_out,
                preferred_element_type=jnp.float32,
            )
        )
    return tuple(results)


def forward_blocks(queries, key_rows, value_rows, key_valid):
    count = queries.shape[0]
    size = min(count, block_rows)
    return level_forward(queries, key_rows, value_rows, key_valid)


def grads_blocks(queries, key_rows, value_rows, key_valid, log_total, grad_out, delta_rows):
    count = queries.shape[0]
    size = min(count, block_rows)
    return level_grads(
        queries, key_rows, value_rows, key_valid, log_total, grad_out, delta_rows, True, True
    )


def per_device(tiles, w_qkv, w_out, cotangent, offsets, pad_count):
    row_count = tiles.shape[0]
    dev_count = lax.axis_size("ctx")
    own_index = lax.axis_index("ctx")
    shaped = (row_count, HEADS, HEAD_DIM)
    packed = jnp.dot(tiles, w_qkv, preferred_element_type=jnp.float32).astype(jnp.bfloat16)
    queries = packed[:, :D].reshape(shaped)
    key_all = packed[:, D : 2 * D].reshape(shaped)
    value_all = packed[:, 2 * D :].reshape(shaped)
    limit = row_count * dev_count - pad_count[0]
    base_pos = own_index * row_count + jnp.arange(row_count, dtype=jnp.int32)
    valid_near = jnp.broadcast_to((base_pos < limit)[None, :], (HEADS, row_count))
    mixed_near, lse_near = forward_blocks(queries, key_all, value_all, valid_near)
    offs_mid = offsets[0]
    mid_rows = row_count // GROUP
    query_mid = pick_rows(queries, GROUP, offs_mid)
    key_mid = pick_rows(key_all, GROUP, offs_mid)
    value_mid = pick_rows(value_all, GROUP, offs_mid)
    gathered = jnp.stack([key_mid.reshape(mid_rows, D), value_mid.reshape(mid_rows, D)])
    bit_total = GROUP.bit_length() - 1
    for bit_index in range(bit_total):
        partner = from_partner(gathered, "ctx", bit_index)
        upper = own_index // 2**bit_index % 2 == 1
        gathered = jnp.where(
            upper,
            jnp.concatenate([partner, gathered], axis=1),
            jnp.concatenate([gathered, partner], axis=1),
        )
    keys_group = gathered[0].reshape(shaped)
    values_group = gathered[1].reshape(shaped)
    group_start = own_index // GROUP * GROUP * row_count
    mid_pos = (
        group_start + jnp.arange(row_count, dtype=jnp.int32)[:, None] * GROUP + offs_mid[None, :]
    )
    valid_mid = (mid_pos < limit).T
    mixed_mid, lse_mid = level_forward(query_mid, keys_group, values_group, valid_mid)
    offs_far = offsets[1]
    far_rows = row_count // dev_count
    query_far = pick_rows(queries, dev_count, offs_far)
    key_far = pick_rows(key_all, dev_count, offs_far)
    value_far = pick_rows(value_all, dev_count, offs_far)
    far_all = lax.all_gather(
        jnp.stack([key_far.reshape(far_rows, D), value_far.reshape(far_rows, D)]),
        "ctx",
        axis=1,
        tiled=True,
    )
    keys_far_all = far_all[0].reshape(shaped)
    values_far_all = far_all[1].reshape(shaped)
    far_pos = jnp.arange(row_count, dtype=jnp.int32)[:, None] * dev_count + offs_far[None, :]
    valid_far = (far_pos < limit).T
    mixed_far, lse_far = level_forward(query_far, keys_far_all, values_far_all, valid_far)
    lse_mid_all = spread_rows(lse_mid, GROUP, offs_mid, -jnp.inf)
    lse_far_all = spread_rows(lse_far, dev_count, offs_far, -jnp.inf)
    log_total = jnp.logaddexp(jnp.logaddexp(lse_near, lse_mid_all), lse_far_all)
    combined = jnp.exp(lse_near - log_total)[..., None] * mixed_near
    combined = combined + jnp.exp(lse_mid_all - log_total)[..., None] * spread_rows(
        mixed_mid, GROUP, offs_mid, 0.0
    )
    combined = combined + jnp.exp(lse_far_all - log_total)[..., None] * spread_rows(
        mixed_far, dev_count, offs_far, 0.0
    )
    attn = combined.astype(jnp.bfloat16).reshape(row_count, D)
    out_rows = (
        tiles.astype(jnp.float32) + jnp.dot(attn, w_out, preferred_element_type=jnp.float32)
    ).astype(jnp.bfloat16)
    grad_attn = jnp.dot(cotangent, w_out.T, preferred_element_type=jnp.float32).astype(jnp.bfloat16)
    grad_wout_part = lax.dot_general(
        attn, cotangent, (((0,), (0,)), ((), ())), preferred_element_type=jnp.float32
    )
    grad_heads = grad_attn.reshape(shaped)
    delta_rows = jnp.sum(
        grad_heads.astype(jnp.float32) * attn.reshape(shaped).astype(jnp.float32), axis=-1
    )
    grad_query_near, grad_key_near, grad_value_near = grads_blocks(
        queries, key_all, value_all, valid_near, log_total, grad_heads, delta_rows
    )
    lse_mid_rows = pick_rows(log_total, GROUP, offs_mid)
    grad_mid_rows = pick_rows(grad_heads, GROUP, offs_mid)
    delta_mid_rows = pick_rows(delta_rows, GROUP, offs_mid)
    grad_query_mid, grad_key_group, grad_value_group = level_grads(
        query_mid,
        keys_group,
        values_group,
        valid_mid,
        lse_mid_rows,
        grad_mid_rows,
        delta_mid_rows,
        True,
        True,
    )
    summed = jnp.stack(
        [grad_key_group.reshape(row_count, D), grad_value_group.reshape(row_count, D)]
    )
    for bit_index in reversed(range(bit_total)):
        half = summed.shape[1] // 2
        lower = summed[:, :half]
        higher = summed[:, half:]
        upper = own_index // 2**bit_index % 2 == 1
        outgoing = jnp.where(upper, lower, higher)
        summed = jnp.where(upper, higher, lower) + from_partner(outgoing, "ctx", bit_index)
    grad_key_mid = summed[0].reshape(mid_rows, HEADS, HEAD_DIM)
    grad_value_mid = summed[1].reshape(mid_rows, HEADS, HEAD_DIM)
    lse_far_rows = pick_rows(log_total, dev_count, offs_far)
    grad_far_rows = pick_rows(grad_heads, dev_count, offs_far)
    delta_far_rows = pick_rows(delta_rows, dev_count, offs_far)
    row_block = jnp.stack(
        [query_far.reshape(far_rows, D), grad_far_rows.reshape(far_rows, D)]
    ).astype(jnp.float32)
    stat_block = jnp.stack([lse_far_rows, delta_far_rows])
    rows_all, stats_all = (
        lax.all_gather(row_block, "ctx", axis=1, tiled=True),
        lax.all_gather(stat_block, "ctx", axis=1, tiled=True),
    )
    query_all = rows_all[0].astype(jnp.bfloat16).reshape(shaped)
    grad_all = rows_all[1].astype(jnp.bfloat16).reshape(shaped)
    (grad_query_far,) = level_grads(
        query_far,
        keys_far_all,
        values_far_all,
        valid_far,
        lse_far_rows,
        grad_far_rows,
        delta_far_rows,
        True,
        False,
    )
    own_pos = (own_index * far_rows + jnp.arange(far_rows, dtype=jnp.int32))[
        :, None
    ] * dev_count + offs_far[None, :]
    grad_key_far, grad_value_far = level_grads(
        query_all,
        key_far,
        value_far,
        (own_pos < limit).T,
        stats_all[0],
        grad_all,
        stats_all[1],
        False,
        True,
    )
    grad_query = (
        grad_query_near
        + spread_rows(grad_query_mid, GROUP, offs_mid, 0.0)
        + spread_rows(grad_query_far, dev_count, offs_far, 0.0)
    )
    grad_key = (
        grad_key_near
        + spread_rows(grad_key_mid, GROUP, offs_mid, 0.0)
        + spread_rows(grad_key_far, dev_count, offs_far, 0.0)
    )
    grad_value = (
        grad_value_near
        + spread_rows(grad_value_mid, GROUP, offs_mid, 0.0)
        + spread_rows(grad_value_far, dev_count, offs_far, 0.0)
    )
    grad_packed = jnp.concatenate(
        [
            grad_query.reshape(row_count, D),
            grad_key.reshape(row_count, D),
            grad_value.reshape(row_count, D),
        ],
        axis=1,
    ).astype(jnp.bfloat16)
    grad_tiles = jnp.dot(grad_packed, w_qkv.T, preferred_element_type=jnp.float32).astype(
        jnp.bfloat16
    )
    grad_wqkv_part = lax.dot_general(
        tiles, grad_packed, (((0,), (0,)), ((), ())), preferred_element_type=jnp.float32
    )
    grad_wqkv, grad_wout = (
        lax.psum_scatter(grad_wqkv_part, "ctx", scatter_dimension=0, tiled=True),
        lax.psum_scatter(grad_wout_part, "ctx", scatter_dimension=0, tiled=True),
    )
    return (out_rows, grad_tiles, grad_wqkv, grad_wout)


def solution(mesh):
    return jax.shard_map(
        per_device,
        mesh=mesh,
        in_specs=(P("ctx", None), P(), P(), P("ctx", None), P(), P()),
        out_specs=(P("ctx", None), P("ctx", None), P("ctx", None), P("ctx", None)),
        check_vma=False,
    )
```

profile of v0, /device:TPU:0, one launch (start us, length us, event | category | flops | bytes accessed | tf_op | source)
XLA Modules:
  0.0 557.5 jit_solution(5915493366938448926)
XLA Ops:
  8.1 2.8 convolution_convert_fusion.2
  10.9 2.4 reshape_reshape.30
  13.3 2.1 convolution_convert_fusion
  16.5 2.5 reshape_reshape.25
  19.0 2.4 reshape_reshape.26
  21.4 2.4 reshape_reshape.24
  23.8 4.6 select_reduce_fusion.1
  35.7 2.4 reshape_reshape.31
  41.9 2.5 reshape_reshape.28
  44.4 2.4 reshape_reshape.29
  46.9 2.4 reshape_reshape.27
  50.6 4.1 select_reduce_fusion
  60.6 45.0 %all_gather.10 = bf16[2,256,768]{2,1,0:T(8,128)(2,1)S(1)} all-gather(bf16[2,8,768]{2,1,0:T(8,128)(2,1)S(1)} %maximum_convert_fusion), channel_id=1, replica_groups=mesh['ctx'=32] {'ctx'}, dimensions={1}, use_global_device_ids=true | all-gather | bytes 811008 | tf_op jit(solution)/shard_map/all_gather | solution.py:216
  106.6 39.1 %all_gather.9 = bf16[2,256,768]{2,1,0:T(8,128)(2,1)S(1)} all-gather(bf16[2,8,768]{2,1,0:T(8,128)(2,1)S(1)} %pad_maximum_fusion.4), channel_id=1, replica_groups=mesh['ctx'=32] {'ctx'}, dimensions={1}, use_global_device_ids=true | all-gather | bytes 811008 | tf_op jit(solution)/shard_map/all_gather | solution.py:146
  151.3 3.5 fusion.85
  181.5 2.0 broadcast_in_dim.374
  183.6 2.8 copy.156
  189.1 2.9 exponential_reduce_fusion
  192.0 6.8 %collective-permute-done.2 = bf16[2,128,768]{2,1,0:T(8,128)(2,1)S(1)} collective-permute-done((bf16[2,128,768]{2,1,0:T(8,128)(2,1)S(1)}, bf16[2,128,768]{2,1,0:T(8,128)(2,1)S(1)}, u32[]{:S(2)}, u32[]{:S(2)}) %collective-permute-start.2) | collective-permute-done | bytes 393248 | tf_op jit(solution)/shard_map/ppermute | solution.py:17
  215.5 2.8 copy.154
  218.2 4.7 multiply_reduce_fusion
  232.2 2.3 fusion.52
  235.4 2.3 copy.168
  238.4 37.4 %all_gather.11 = f32[2,256,12]{2,1,0:T(8,128)S(1)} all-gather(f32[2,8,12]{2,1,0:T(8,128)S(1)} %pad_maximum_fusion.5), channel_id=1, replica_groups=mesh['ctx'=32] {'ctx'}, dimensions={1}, use_global_device_ids=true | all-gather | bytes 25344 | tf_op jit(solution)/shard_map/all_gather | solution.py:217
  279.7 2.2 convolution_multiply_fusion.2
  281.9 2.3 copy.167
  284.2 2.3 broadcast_select_fusion
  286.5 2.1 fusion.49
  290.5 2.1 fusion.46
  297.1 9.6 %collective-permute-done.3 = f32[2,128,768]{2,1,0:T(8,128)} collective-permute-done((f32[2,128,768]{2,1,0:T(8,128)}, f32[2,128,768]{2,1,0:T(8,128)}, u32[]{:S(2)}, u32[]{:S(2)}) %collective-permute-start.3) | collective-permute-done | bytes 786464 | tf_op jit(solution)/shard_map/ppermute | solution.py:17
  312.5 2.8 copy.161
  315.3 2.0 broadcast_in_dim.392
  317.3 2.7 copy.183
  320.1 2.0 broadcast_in_dim.387
  322.1 2.7 copy.179
  324.9 2.0 broadcast_in_dim.380
  326.9 2.8 copy.163
  330.0 3.1 multiply_convert_fusion
  344.6 2.9 copy.182
  347.5 2.2 broadcast_bitcast_fusion.1
  349.7 2.8 copy.170
  352.6 2.8 fusion.30
  355.7 2.3 fusion.27
  358.7 4.0 convolution_bitcast_fusion
  362.7 8.0 %copy.190 = f32[768,2304]{1,0:T(8,128)} copy(f32[768,2304]{0,1:T(8,128)} %convolution_bitcast_fusion) | data formatting | bytes 14155776
  370.8 2.8 fusion.25
  375.6 49.7 %reduce-scatter.5.cloned.1.call-done = f32[24,768]{1,0:T(8,128)} async-done(((f32[768,768]{1,0:T(8,128)}), f32[24,768]{1,0:T(8,128)}) %reduce-scatter.5.cloned.1.call-update) | async-done | bytes 73744 | tf_op jit(solution)/shard_map/reduce_scatter | solution.py:277
  425.2 125.5 %reduce-scatter.7.cloned.1.call-done = f32[24,2304]{1,0:T(8,128)} async-done(((f32[768,2304]{1,0:T(8,128)}), f32[24,2304]{1,0:T(8,128)}) %reduce-scatter.7.cloned.1.call-update) | async-done | bytes 221200
  (182 shorter events, 113.8 us)
Async XLA Ops:
  7.2 6.2 %copy-start = (bf16[768,2304]{1,0:T(8,128)(2,1)S(1)}, bf16[768,2304]{1,0:T(8,128)(2,1)}, u32[]{:S(2)}) copy-start(bf16[768,2304]{1,0:T(8,128)(2,1)} %param.7) | copy-start | bytes 10616836
  7.2 418.0 %reduce-scatter.5.cloned.1.call-start = ((), (), s32[]{:S(2)}) async-start(), calls=%async_computation.2 | async-start | bytes 2433024 | tf_op jit(solution)/shard_map/reduce_scatter | solution.py:277
  8.1 5.3 copy-start.36
  8.1 140.5 %copy-start.34 = (s32[12]{0:T(128)}, s32[12]{0:T(128)S(1)}, u32[]{:S(2)}) copy-start(s32[12]{0:T(128)S(1)} %get-tuple-element.55) | copy-start | bytes 148
  8.1 15.8 %copy-start.35 = (pred[8,12]{1,0:T(8,128)(4,1)}, pred[8,12]{1,0:T(8,128)(4,1)S(1)}, u32[]{:S(2)}) copy-start(pred[8,12]{1,0:T(8,128)(4,1)S(1)} %iota_compare_fusion.1) | copy-start | bytes 292
  34.6 122.8 %collective-permute-start = (bf16[2,32,768]{2,1,0:T(8,128)(2,1)}, bf16[2,32,768]{2,1,0:T(8,128)(2,1)}, u32[]{:S(2)}, u32[]{:S(2)}) collective-permute-start(bf16[2,32,768]{2,1,0:T(8,128)(2,1)} %constant_dynamic-update-slice_fusion), channel_id=1, source_target_pairs={{0,1},{1,0},{2,3},{3,2},{4,5},{5,4},{6,7},{7,6},{8,9},{9,8},{10,11... | collective-permute-start | bytes 294920 | tf_op jit(solution)/shard_map/ppermute | solution.py:17
  50.6 4.2 copy-start.32
  59.9 46.7 %copy-start.31 = (bf16[1,8,768]{2,1,0:T(8,128)(2,1)S(1)}, bf16[1,8,768]{2,1,0:T(8,128)(2,1)}, u32[]{:S(2)}) copy-start(bf16[1,8,768]{2,1,0:T(8,128)(2,1)} %stack_reshape.27) | copy-start | bytes 36868
  106.6 42.0 %copy-start.37 = (s32[12]{0:T(128)S(1)}, s32[12]{0:T(128)}, u32[]{:S(2)}) copy-start(s32[12]{0:T(128)} %copy-done.36) | copy-start | bytes 148
  106.6 42.0 %copy-start.38 = (s32[256]{0:T(256)S(1)}, s32[256]{0:T(256)}, u32[]{:S(2)}) copy-start(s32[256]{0:T(256)} %iota_multiply_fusion) | copy-start | bytes 3076
  106.6 42.0 %copy-start.39 = (s32[256]{0:T(256)S(1)}, s32[256]{0:T(256)}, u32[]{:S(2)}) copy-start(s32[256]{0:T(256)} %multiply_add_fusion) | copy-start | bytes 3076
  150.5 0.6 copy-start.20
  154.8 34.2 %copy-start.29 = (f32[12,256]{1,0:T(8,128)}, f32[12,256]{1,0:T(8,128)S(1)}, u32[]{:S(2)}) copy-start(f32[12,256]{1,0:T(8,128)S(1)} %get-tuple-element.60) | copy-start | bytes 36868
  159.1 27.2 %collective-permute-start.1 = (bf16[2,64,768]{2,1,0:T(8,128)(2,1)}, bf16[2,64,768]{2,1,0:T(8,128)(2,1)}, u32[]{:S(2)}, u32[]{:S(2)}) collective-permute-start(bf16[2,64,768]{2,1,0:T(8,128)(2,1)} %maximum_select_fusion.2), channel_id=1, source_target_pairs={{0,2},{1,3},{2,0},{3,1},{4,6},{5,7},{6,4},{7,5},{8,10},{9,11},{10,... | collective-permute-start | bytes 589832 | tf_op jit(solution)/shard_map/ppermute | solution.py:17
  187.7 11.1 %collective-permute-start.2 = (bf16[2,128,768]{2,1,0:T(8,128)(2,1)S(1)}, bf16[2,128,768]{2,1,0:T(8,128)(2,1)S(1)}, u32[]{:S(2)}, u32[]{:S(2)}) collective-permute-start(bf16[2,128,768]{2,1,0:T(8,128)(2,1)S(1)} %maximum_select_fusion.1), channel_id=1, source_target_pairs={{0,4},{1,5},{2,6},{3,7},{4,0},{5,1},{6,2},{7,3},{8,12},{9,13},{10,... | collective-permute-start | bytes 1179656 | tf_op jit(solution)/shard_map/ppermute | solution.py:17
  199.1 2.9 copy-start.33
  203.3 0.7 copy-start.3
  204.3 0.6 copy-start.30
  230.9 3.6 copy-start.4
  230.9 3.6 copy-start.9
  230.9 3.6 copy-start.23
  286.5 20.1 %collective-permute-start.3 = (f32[2,128,768]{2,1,0:T(8,128)}, f32[2,128,768]{2,1,0:T(8,128)}, u32[]{:S(2)}, u32[]{:S(2)}) collective-permute-start(f32[2,128,768]{2,1,0:T(8,128)} %broadcast_select_fusion), channel_id=1, source_target_pairs={{0,4},{1,5},{2,6},{3,7},{4,0},{5,1},{6,2},{7,3},{8,12},{9,13},{10,... | collective-permute-start | bytes 2359304 | tf_op jit(solution)/shard_map/ppermute | solution.py:17
  292.6 2.6 copy-start.13
  292.6 2.6 copy-start.21
  297.1 14.6 %copy-start.8 = (bf16[1,256,768]{1,2,0:T(8,128)(2,1)S(1)}, bf16[1,256,768]{1,2,0:T(8,128)(2,1)}, u32[]{:S(2)}) copy-start(bf16[1,256,768]{1,2,0:T(8,128)(2,1)} %copy.176) | copy-start | bytes 1179652
  297.1 14.6 %copy-start.22 = (f32[12,256,8]{1,2,0:T(8,128)S(1)}, f32[12,256,8]{1,2,0:T(8,128)}, u32[]{:S(2)}) copy-start(f32[12,256,8]{1,2,0:T(8,128)} %fusion.41) | copy-start | bytes 294916
  308.4 0.9 copy-start.5
  310.1 23.1 %collective-permute-start.4 = (f32[2,64,768]{2,1,0:T(8,128)}, f32[2,64,768]{2,1,0:T(8,128)}, u32[]{:S(2)}, u32[]{:S(2)}) collective-permute-start(f32[2,64,768]{2,1,0:T(8,128)} %slice_select_fusion), channel_id=1, source_target_pairs={{0,2},{1,3},{2,0},{3,1},{4,6},{5,7},{6,4},{7,5},{8,10},{9,11},{10,... | collective-permute-start | bytes 1179656 | tf_op jit(solution)/shard_map/ppermute | solution.py:17
  329.8 220.9 %reduce-scatter.7.cloned.1.call-start = ((), (), s32[]{:S(2)}) async-start(), calls=%async_computation.3 | async-start | bytes 7299072
  330.0 3.1 copy-start.6
  333.1 3.4 copy-start.2
  333.1 1.9 copy-start.10
  333.1 1.9 copy-start.11
  333.1 2.2 copy-start.12
  333.1 2.2 copy-start.25
  333.2 2.2 copy-start.27
  334.9 1.6 collective-permute-start.5
  352.5 3.1 copy-start.1
  352.6 3.1 copy-start.7
  352.6 3.1 copy-start.26
  352.6 3.1 copy-start.28
  355.7 2.3 copy-start.16
  355.7 3.0 copy-start.14
  355.7 3.0 copy-start.24
  357.9 0.8 copy-start.18
  370.8 2.8 copy-start.15
  370.8 2.8 copy-start.17
  370.8 2.8 copy-start.19
Sparse Core Ops, SparseCore 0:
  329.9 95.2 reduce-scatter.4
  432.4 118.2 reduce-scatter.6
where the time goes:
time: 561 us; the launch traced here: 558 us
  waiting for transfers between devices  192 us (34%)
  local copies, waits for them, and re-layouts  140 us (25%)
  blocking collectives  121 us (22%)
  matrix products  52.5 us (9%)
  other arithmetic  32.9 us (6%)
  between operations  15.1 us (3%)
    unnamed x3, waiting for transfers between devices  126 us
    broadcast_in_dim x28, local copies, waits for them, and re-layouts, spread_rows(): jnp.where(chosen, array_in[:, None], jnp.asarray(fill, array_in.dtype))  53.5 us
    reduce_scatter x1, waiting for transfers between devices, per_device(): lax.psum_scatter(grad_wout_part, 'ctx', scatter_dimension=0, tiled=True)  49.7 us
    all_gather x1, blocking collectives, per_device(): lax.all_gather(row_block, 'ctx', axis=1, tiled=True)  45 us
    all_gather x1, blocking collectives, per_device(): lax.all_gather(jnp.stack([key_far.reshape(far_rows, D), value_far.reshape...  39.1 us
    all_gather x1, blocking collectives, per_device(): lax.all_gather(stat_block, 'ctx', axis=1, tiled=True)  37.4 us
    another operation x8, local copies, waits for them, and re-layouts, pick_rows(): array_in.reshape((row_count // stride, stride) + array_in.shape[1:])  19.6 us
    ppermute x6, waiting for transfers between devices, from_partner(): return lax.ppermute(value, axis, pairs)  16.4 us
  transfers between devices with their start and end apart: 8, of which 4 were waited for; matrix products, arithmetic and copies ran while one was open for 25% of the time, Pallas kernels for 0%

commit v1 on v0

--- a/solution.py
+++ b/solution.py
@@ -9,6 +9,33 @@
 GROUP = 8
 scale_factor = 0.125
 block_rows = 512
+
+
+def settle_the_lane(t0, d_out):
+    t0 = jnp.moveaxis(t0, 0, d_out)
+    y = t0.shape
+    value_now = t0.reshape(*y[:d_out], y[d_out] * y[d_out + 1], *y[d_out + 2 :])
+    return value_now
+
+
+def lots_all_advance(m, ax_name):
+    world = lax.axis_size(ax_name)
+    mat_out = m[None]
+    for j in range(world.bit_length() - 1):
+        opened = 1 << j
+        all_rows = []
+        for ix in range(world):
+            all_rows.append((ix, ix ^ opened))
+        carry_out = lax.ppermute(mat_out, ax_name, all_rows)
+        y1 = jnp.stack([mat_out, carry_out])
+        response = lax.axis_index(ax_name) >> j & 1
+        mat_out = jnp.where(response == 0, y1, y1[::-1]).reshape(-1, *m.shape)
+    return mat_out
+
+
+def try_all_point(arr, unit, out_dim):
+    piece_next = settle_the_lane(lots_all_advance(arr, unit), out_dim)
+    return piece_next
 
 
 def from_partner(value, axis, apart):
@@ -143,11 +170,8 @@
     query_far = pick_rows(queries, dev_count, offs_far)
     key_far = pick_rows(key_all, dev_count, offs_far)
     value_far = pick_rows(value_all, dev_count, offs_far)
-    far_all = lax.all_gather(
-        jnp.stack([key_far.reshape(far_rows, D), value_far.reshape(far_rows, D)]),
-        "ctx",
-        axis=1,
-        tiled=True,
+    far_all = try_all_point(
+        jnp.stack([key_far.reshape(far_rows, D), value_far.reshape(far_rows, D)]), "ctx", 1
     )
     keys_far_all = far_all[0].reshape(shaped)
     values_far_all = far_all[1].reshape(shaped)

time: 561 us -> 530 us (0.945)
  blocking collectives: 121 us -> 84.6 us
    all_gather x1 -> x0, blocking collectives: 39.1 us -> none  [per_device(): lax.all_gather(jnp.stack([key_far.reshape(far_rows, D), value_far.reshape...]
    another operation x0 -> x4, local copies, waits for them, and re-layouts: none -> 10 us  [the longest x2 5.03 us: per_device(): keys_far_all = far_all[0].reshape(shaped)]
    ppermute x0 -> x5, waiting for transfers between devices: none -> 7.62 us  [lots_all_advance(): carry_out = lax.ppermute(mat_out, ax_name, all_rows)]
    unnamed x82 -> x95, local copies, waits for them, and re-layouts: 13.9 us -> 15 us
  transfers between devices with their start and end apart: 8 -> 13, of which waited for: 4 -> 6; matrix products, arithmetic and copies ran while one was open for 25% -> 27% of each run, Pallas kernels for 0% -> 0%
where the time goes in v1:
time: 530 us; the launch traced here: 527 us
  waiting for transfers between devices  196 us (37%)
  local copies, waits for them, and re-layouts  144 us (27%)
  blocking collectives  84.6 us (16%)
  matrix products  48.5 us (9%)
  other arithmetic  35.7 us (7%)
  between operations  15.3 us (3%)
    unnamed x3, waiting for transfers between devices  125 us
    reduce_scatter x1, waiting for transfers between devices, per_device(): lax.psum_scatter(grad_wout_part, 'ctx', scatter_dimension=0, tiled=True)  51.3 us
    broadcast_in_dim x28, local copies, waits for them, and re-layouts, spread_rows(): jnp.where(chosen, array_in[:, None], jnp.asarray(fill, array_in.dtype))  51 us
    all_gather x1, blocking collectives, per_device(): lax.all_gather(row_block, 'ctx', axis=1, tiled=True)  45.5 us
    all_gather x1, blocking collectives, per_device(): lax.all_gather(stat_block, 'ctx', axis=1, tiled=True)  39.1 us
    another operation x8, local copies, waits for them, and re-layouts, pick_rows(): array_in.reshape((row_count // stride, stride) + array_in.shape[1:])  19.5 us
    unnamed x95, local copies, waits for them, and re-layouts  15 us
    reduce_sum x4, other arithmetic, pick_rows(): jnp.sum(jnp.where(chosen, blocked, jnp.zeros((), array_in.dtype)), axis=1)  11.6 us
  transfers between devices with their start and end apart: 13, of which 6 were waited for; matrix products, arithmetic and copies ran while one was open for 27% of the time, Pallas kernels for 0%

profile of v1, /device:TPU:0, one launch (start us, length us, event | category | flops | bytes accessed | tf_op | source)
XLA Modules:
  0.0 526.6 jit_solution(13658230121975541549)
XLA Ops:
  9.2 2.6 convolution_convert_fusion.2
  11.8 2.4 reshape_reshape.31
  14.2 2.1 convolution_convert_fusion
  17.4 2.4 reshape_reshape.28
  19.8 2.4 reshape_reshape.29
  22.2 2.4 reshape_reshape.27
  24.7 4.1 select_reduce_fusion
  32.2 2.4 reshape_reshape.30
  34.6 2.4 reshape_reshape.25
  37.0 2.4 reshape_reshape.26
  39.5 2.4 reshape_reshape.24
  41.9 4.6 select_reduce_fusion.1
  61.5 45.5 %all_gather.6 = bf16[2,256,768]{2,1,0:T(8,128)(2,1)S(1)} all-gather(bf16[2,8,768]{2,1,0:T(8,128)(2,1)S(1)} %maximum_convert_fusion), channel_id=1, replica_groups=mesh['ctx'=32] {'ctx'}, dimensions={1}, use_global_device_ids=true | all-gather | bytes 811008 | tf_op jit(solution)/shard_map/all_gather | solution.py:240
  112.6 4.4 collective-permute-done.4
  119.2 3.3 collective-permute-done.5
  154.8 2.2 broadcast_bitcast_fusion.3
  157.0 2.8 copy.169
  162.0 2.4 reshape_squeeze.13
  164.5 2.6 copy.165
  175.4 2.4 reshape_squeeze.15
  177.8 2.6 copy.170
  183.0 2.8 copy.171
  185.8 4.7 multiply_reduce_fusion
  199.7 2.3 fusion.52
  202.9 2.3 copy.185
  205.9 39.1 %all_gather.7 = f32[2,256,12]{2,1,0:T(8,128)S(1)} all-gather(f32[2,8,12]{2,1,0:T(8,128)S(1)} %pad_maximum_fusion.9), channel_id=1, replica_groups=mesh['ctx'=32] {'ctx'}, dimensions={1}, use_global_device_ids=true | all-gather | bytes 25344 | tf_op jit(solution)/shard_map/all_gather | solution.py:241
  248.9 2.2 convolution_multiply_fusion.2
  251.1 2.3 copy.184
  253.4 2.3 broadcast_select_fusion
  255.8 2.1 fusion.49
  259.7 2.1 fusion.46
  266.3 9.5 %collective-permute-done.8 = f32[2,128,768]{2,1,0:T(8,128)} collective-permute-done((f32[2,128,768]{2,1,0:T(8,128)}, f32[2,128,768]{2,1,0:T(8,128)}, u32[]{:S(2)}, u32[]{:S(2)}) %collective-permute-start.8) | collective-permute-done | bytes 786464 | tf_op jit(solution)/shard_map/ppermute | solution.py:44
  280.3 2.8 copy.176
  283.0 2.1 broadcast_in_dim.396
  285.1 2.8 copy.200
  289.9 2.7 copy.196
  294.7 2.8 copy.180
  297.6 3.0 multiply_convert_fusion
  312.1 2.8 copy.199
  315.0 2.2 broadcast_bitcast_fusion.1
  317.2 2.8 copy.187
  320.0 2.8 fusion.30
  323.2 2.2 fusion.27
  326.2 4.0 convolution_bitcast_fusion
  330.2 8.1 %copy.207 = f32[768,2304]{1,0:T(8,128)} copy(f32[768,2304]{0,1:T(8,128)} %convolution_bitcast_fusion) | data formatting | bytes 14155776
  338.3 2.8 fusion.25
  343.1 51.3 %reduce-scatter.5.cloned.1.call-done = f32[24,768]{1,0:T(8,128)} async-done(((f32[768,768]{1,0:T(8,128)}), f32[24,768]{1,0:T(8,128)}) %reduce-scatter.5.cloned.1.call-update) | async-done | bytes 73744 | tf_op jit(solution)/shard_map/reduce_scatter | solution.py:301
  394.4 125.4 %reduce-scatter.7.cloned.1.call-done = f32[24,2304]{1,0:T(8,128)} async-done(((f32[768,2304]{1,0:T(8,128)}), f32[24,2304]{1,0:T(8,128)}) %reduce-scatter.7.cloned.1.call-update) | async-done | bytes 221200
  (217 shorter events, 117.8 us)
Async XLA Ops:
  7.2 7.1 %copy-start = (bf16[768,2304]{1,0:T(8,128)(2,1)S(1)}, bf16[768,2304]{1,0:T(8,128)(2,1)}, u32[]{:S(2)}) copy-start(bf16[768,2304]{1,0:T(8,128)(2,1)} %param.7) | copy-start | bytes 10616836
  7.2 387.2 %reduce-scatter.5.cloned.1.call-start = ((), (), s32[]{:S(2)}) async-start(), calls=%async_computation.2 | async-start | bytes 2433024 | tf_op jit(solution)/shard_map/reduce_scatter | solution.py:301
  31.7 79.4 %collective-permute-start.3 = (bf16[1,2,8,768]{3,2,1,0:T(8,128)(2,1)}, bf16[1,2,8,768]{3,2,1,0:T(8,128)(2,1)}, u32[]{:S(2)}, u32[]{:S(2)}) collective-permute-start(bf16[1,2,8,768]{3,2,1,0:T(8,128)(2,1)} %bitcast.238), channel_id=1, source_target_pairs={{0,1},{1,0},{2,3},{3,2},{4,5},{5,4},{6,7},{7,6},{8,9},{9,8},{10,11... | collective-permute-start | bytes 73736 | tf_op jit(solution)/shard_map/ppermute | solution.py:29
  37.0 4.9 copy-start.42
  41.9 4.7 copy-start.40
  52.7 65.2 %collective-permute-start = (bf16[2,32,768]{2,1,0:T(8,128)(2,1)}, bf16[2,32,768]{2,1,0:T(8,128)(2,1)}, u32[]{:S(2)}, u32[]{:S(2)}) collective-permute-start(bf16[2,32,768]{2,1,0:T(8,128)(2,1)} %constant_dynamic-update-slice_fusion), channel_id=1, source_target_pairs={{0,1},{1,0},{2,3},{3,2},{4,5},{5,4},{6,7},{7,6},{8,9},{9,8},{10,11... | collective-permute-start | bytes 294920 | tf_op jit(solution)/shard_map/ppermute | solution.py:44
  60.7 47.3 %copy-start.12 = (bf16[256,768]{0,1:T(8,128)(2,1)S(1)}, bf16[256,768]{0,1:T(8,128)(2,1)}, u32[]{:S(2)}) copy-start(bf16[256,768]{0,1:T(8,128)(2,1)} %copy.156) | copy-start | bytes 1179652
  60.7 47.3 %copy-start.13 = (bf16[256,768]{0,1:T(8,128)(2,1)S(1)}, bf16[256,768]{0,1:T(8,128)(2,1)}, u32[]{:S(2)}) copy-start(bf16[256,768]{0,1:T(8,128)(2,1)} %copy.157) | copy-start | bytes 1179652
  108.8 1.6 copy-start.1
  110.4 17.8 %copy-start.41 = (pred[8,12]{1,0:T(8,128)(4,1)S(1)}, pred[8,12]{1,0:T(8,128)(4,1)}, u32[]{:S(2)}) copy-start(pred[8,12]{1,0:T(8,128)(4,1)} %copy-done.40) | copy-start | bytes 292
  112.5 4.4 collective-permute-start.4
  117.8 4.7 collective-permute-start.5
  119.0 6.1 %collective-permute-start.1 = (bf16[2,64,768]{2,1,0:T(8,128)(2,1)S(1)}, bf16[2,64,768]{2,1,0:T(8,128)(2,1)S(1)}, u32[]{:S(2)}, u32[]{:S(2)}) collective-permute-start(bf16[2,64,768]{2,1,0:T(8,128)(2,1)S(1)} %maximum_select_fusion.2), channel_id=1, source_target_pairs={{0,2},{1,3},{2,0},{3,1},{4,6},{5,7},{6,4},{7,5},{8,10},{9,11},{10,... | collective-permute-start | bytes 589832 | tf_op jit(solution)/shard_map/ppermute | solution.py:44
  123.2 17.7 %collective-permute-start.6 = (bf16[8,2,8,768]{3,2,1,0:T(8,128)(2,1)}, bf16[8,2,8,768]{3,2,1,0:T(8,128)(2,1)}, u32[]{:S(2)}, u32[]{:S(2)}) collective-permute-start(bf16[8,2,8,768]{3,2,1,0:T(8,128)(2,1)} %bitcast.18), channel_id=1, source_target_pairs={{0,8},{1,9},{2,10},{3,11},{4,12},{5,13},{6,14},{7,15},{8,0},{9,1},... | collective-permute-start | bytes 589832 | tf_op jit(solution)/shard_map/ppermute | solution.py:29
  125.9 17.0 %collective-permute-start.2 = (bf16[2,128,768]{2,1,0:T(8,128)(2,1)}, bf16[2,128,768]{2,1,0:T(8,128)(2,1)}, u32[]{:S(2)}, u32[]{:S(2)}) collective-permute-start(bf16[2,128,768]{2,1,0:T(8,128)(2,1)} %maximum_select_fusion.1), channel_id=1, source_target_pairs={{0,4},{1,5},{2,6},{3,7},{4,0},{5,1},{6,2},{7,3},{8,12},{9,13},{10,... | collective-permute-start | bytes 1179656 | tf_op jit(solution)/shard_map/ppermute | solution.py:44
  129.6 3.8 copy-start.35
  142.9 16.9 %collective-permute-start.7 = (bf16[16,2,8,768]{3,2,0,1:T(8,128)(2,1)}, bf16[16,2,8,768]{3,2,0,1:T(8,128)(2,1)}, u32[]{:S(2)}, u32[]{:S(2)}) collective-permute-start(bf16[16,2,8,768]{3,2,0,1:T(8,128)(2,1)} %bitcast.21), channel_id=1, source_target_pairs={{0,16},{1,17},{2,18},{3,19},{4,20},{5,21},{6,22},{7,23},{8,24},{9,... | collective-permute-start | bytes 1179656 | tf_op jit(solution)/shard_map/ppermute | solution.py:29
  144.4 4.8 copy-start.37
  149.2 2.2 copy-start.10
  162.0 5.0 copy-start.36
  198.4 3.6 copy-start.5
  198.4 3.6 copy-start.11
  198.4 3.6 copy-start.27
  255.8 20.1 %collective-permute-start.8 = (f32[2,128,768]{2,1,0:T(8,128)}, f32[2,128,768]{2,1,0:T(8,128)}, u32[]{:S(2)}, u32[]{:S(2)}) collective-permute-start(f32[2,128,768]{2,1,0:T(8,128)} %broadcast_select_fusion), channel_id=1, source_target_pairs={{0,4},{1,5},{2,6},{3,7},{4,0},{5,1},{6,2},{7,3},{8,12},{9,13},{10,... | collective-permute-start | bytes 2359304 | tf_op jit(solution)/shard_map/ppermute | solution.py:44
  261.8 2.6 copy-start.17
  261.8 2.6 copy-start.25
  266.3 13.1 %copy-start.9 = (bf16[1,256,768]{1,2,0:T(8,128)(2,1)S(1)}, bf16[1,256,768]{1,2,0:T(8,128)(2,1)}, u32[]{:S(2)}) copy-start(bf16[1,256,768]{1,2,0:T(8,128)(2,1)} %copy.193) | copy-start | bytes 1179652
  266.3 13.1 %copy-start.26 = (f32[12,256,8]{1,2,0:T(8,128)S(1)}, f32[12,256,8]{1,2,0:T(8,128)}, u32[]{:S(2)}) copy-start(f32[12,256,8]{1,2,0:T(8,128)} %fusion.41) | copy-start | bytes 294916
  279.3 21.4 %collective-permute-start.9 = (f32[2,64,768]{2,1,0:T(8,128)}, f32[2,64,768]{2,1,0:T(8,128)}, u32[]{:S(2)}, u32[]{:S(2)}) collective-permute-start(f32[2,64,768]{2,1,0:T(8,128)} %slice_select_fusion), channel_id=1, source_target_pairs={{0,2},{1,3},{2,0},{3,1},{4,6},{5,7},{6,4},{7,5},{8,10},{9,11},{10,... | collective-permute-start | bytes 1179656 | tf_op jit(solution)/shard_map/ppermute | solution.py:44
  297.5 222.2 %reduce-scatter.7.cloned.1.call-start = ((), (), s32[]{:S(2)}) async-start(), calls=%async_computation.3 | async-start | bytes 7299072
  297.6 3.1 copy-start.7
  300.6 3.4 copy-start.3
  300.6 1.8 copy-start.14
  300.6 1.9 copy-start.15
  300.7 2.2 copy-start.16
  300.7 2.2 copy-start.29
  300.7 2.2 copy-start.31
  302.4 1.6 collective-permute-start.10
  320.0 3.1 copy-start.2
  320.0 3.1 copy-start.8
  320.0 3.1 copy-start.30
  320.0 3.1 copy-start.32
  323.1 2.3 copy-start.20
  323.1 3.0 copy-start.18
  323.1 3.0 copy-start.28
  338.3 2.9 copy-start.19
  338.3 2.8 copy-start.21
  338.3 2.8 copy-start.23
  (11 other events, 12.3 us)
Sparse Core Ops, SparseCore 0:
  297.7 96.6 reduce-scatter.4
  401.6 118.1 reduce-scatter.6
